TPU v7x, 256 devices: a whole 4x4x8 slice. The times are simulated.
256 devices in a mesh: dp: 16 (over z, core), tensor: 16 (over y, x).
Axes of the slice: x: 4, y: 4, z: 8, core: 2. Of those that a mesh axis runs over, the one named last changes fastest.
Arguments:
- activations: bfloat16 [36864, 8192], P('dp', 'tensor'), may hold values from -6 to 6
- out_grads: bfloat16 [36864, 28672], P('dp', 'tensor'), may hold values from -0.0546875 to 0.0546875
- basis: bfloat16 [8192, 256], P('tensor'), may hold values from -0.375 to 0.375
- first_moment: float32 [256, 28672], P('dp', 'tensor'), may hold values from -6 to 6
- second_moment: float32 [256, 28672], P('dp', 'tensor'), may hold values from 0.05 to 0.8
- reward_codes: int32 [36864], P('dp'), may hold values from 0 to 15
- token_ids: int32 [36864], P('dp'), may hold values from 0 to 128004, as said below
Outputs:
- new_first: float32 [256, 28672], P('dp', 'tensor')
- new_second: float32 [256, 28672], P('dp', 'tensor')
- weight_update: bfloat16 [8192, 28672], P('dp', 'tensor')
Inputs may be any that keep to these rules, and one draw needn't show every extreme that they name: `token_ids`: the id 128004 is the padding token; the first of each 2304 consecutive tokens is never padding.
All inputs are finite; a program needn't handle non-finite values.
Results may differ from a plain program's by a relative error of at most 0.019.
Values may be sent and summed in bfloat16 or wider, within the bound.
A program may use at most 64 MiB of HBM per device.

v0:
```python
import jax
import jax.numpy as jnp
from jax import lax
from jax.sharding import PartitionSpec as P

ADAM_STEP = 100


pad_token = 128004
reward_temp = 0.2
beta_one = 0.9
beta_two = 0.999
adam_eps = 1e-08


def filled_up(lines, size):
    spare = -len(lines) % size
    return jnp.pad(lines, [(0, spare)] + [(0, 0)] * (lines.ndim - 1))


def joined_along(parts, dim):
    parts = jnp.moveaxis(parts, 0, dim)
    lengths = parts.shape
    return parts.reshape(*lengths[:dim], lengths[dim] * lengths[dim + 1], *lengths[dim + 2 :])


def sent_to_all(shard, axis):
    size = lax.axis_size(axis)
    return lax.all_to_all(
        jnp.broadcast_to(shard[None], (size, *shard.shape)), axis, 0, 0, tiled=True
    )


def gather_directly(shard, axis, dim):
    return joined_along(sent_to_all(shard, axis), dim)


def split_up(shard, dim, size):
    before, after = (shard.shape[:dim], shard.shape[dim + 1 :])
    return jnp.moveaxis(shard.reshape(*before, size, -1, *after), dim, 0)


def sum_at_owner(shard, axis, dim):
    parts = split_up(shard, dim, lax.axis_size(axis))
    arrived = lax.all_to_all(parts, axis, split_axis=0, concat_axis=0, tiled=True)
    return arrived.astype(jnp.float32).sum(axis=0)


def total_of(shard, axes):
    lines = shard.reshape(-1, shard.shape[-1])
    padded = filled_up(lines, lax.axis_size(axes))
    whole = gather_directly(sum_at_owner(padded, axes, 0).astype(jnp.bfloat16), axes, 0)
    return lax.slice_in_dim(whole, 0, len(lines)).reshape(shard.shape).astype(jnp.float32)


def of_everyone(shard, axis):
    return sent_to_all(shard, axis).sum(axis=0)


def broadcast(shard, axis, root):
    return lax.dynamic_index_in_dim(lax.all_gather(shard, axis), root, 0, keepdims=False)


def local(activations, out_grads, basis, first_moment, second_moment, reward_codes, token_ids):
    data_count = lax.axis_size("dp")
    tensor_count = lax.axis_size("tensor")
    partial_value = jnp.dot(activations, basis, preferred_element_type=jnp.float32)
    projected = total_of(partial_value.astype(jnp.bfloat16), "tensor")
    unmasked = (token_ids != pad_token).astype(jnp.float32)
    weights = unmasked * jnp.exp(reward_temp * reward_codes.astype(jnp.float32))
    local_total = jnp.sum(weights)
    weighted = (weights[:, None] * projected).astype(jnp.bfloat16)
    raw_grad = lax.dot_general(
        weighted, out_grads, (((0,), (0,)), ((), ())), preferred_element_type=jnp.float32
    )
    normalizer = of_everyone(local_total, "dp")
    grad_rows = sum_at_owner(raw_grad.astype(jnp.bfloat16), "dp", 0)
    token_count = activations.shape[0] * data_count
    gradient = grad_rows * (token_count / normalizer)
    new_first = beta_one * first_moment + (1.0 - beta_one) * gradient
    new_second = beta_two * second_moment + (1.0 - beta_two) * gradient * gradient
    bias_one = 1.0 - beta_one**ADAM_STEP
    bias_two = 1.0 - beta_two**ADAM_STEP
    update = (new_first / bias_one / (jnp.sqrt(new_second / bias_two) + adam_eps)).astype(
        jnp.bfloat16
    )
    data_index = lax.axis_index("dp")
    owner_index = data_index * tensor_count // data_count
    owner_rows = broadcast(basis, "tensor", owner_index)
    summed = jnp.dot(
        owner_rows,
        lax.all_gather(update, "dp", axis=0, tiled=True),
        preferred_element_type=jnp.float32,
    )
    return (new_first, new_second, summed.astype(jnp.bfloat16))


def solution(mesh):
    return jax.shard_map(
        local,
        mesh=mesh,
        in_specs=(
            P("dp", "tensor"),
            P("dp", "tensor"),
            P("tensor", None),
            P("dp", "tensor"),
            P("dp", "tensor"),
            P("dp"),
            P("dp"),
        ),
        out_specs=(P("dp", "tensor"), P("dp", "tensor"), P("dp", "tensor")),
        check_vma=False,
    )
```

profile of v0, /device:TPU:1, one launch (start us, length us, event | category | flops | bytes accessed | tf_op | source)
XLA Modules:
  0.0 148.8 jit_solution(3367582259047807124)
XLA Ops:
  7.2 0.0 copy-start
  7.2 0.0 all-gather.3.cloned.1.call-start
  7.2 0.7 all-gather.3.cloned.1.call-update
  7.9 0.9 copy-done
  8.8 1.7 %convolution_convert_fusion = bf16[2304,256]{1,0:T(8,128)(2,1)S(1)} fusion(bf16[2304,512]{1,0:T(8,128)(2,1)S(1)} %copy-done, bf16[512,256]{1,0:T(8,128)(2,1)} %param.9), kind=kOutput, calls=%fused_computation | convolution fusion | flops 604569600 | bytes 3801088 | tf_op jit(solution)/shard_map/dot_general | solution.py:67
  10.6 26.5 %all_to_all.21 = bf16[16,144,256]{2,1,0:T(8,128)(2,1)S(1)} all-to-all(bf16[16,144,256]{2,1,0:T(8,128)(2,1)S(1)} %bitcast.14), channel_id=1, replica_groups=mesh['dp'=16,'tensor'=16] {'tensor'}, dimensions={0} | all-to-all | bytes 2359296 | tf_op jit(solution)/shard_map/all_to_all | solution.py:45
  37.1 0.8 reduce_sum.39
  37.9 2.0 %broadcast_in_dim.4 = bf16[16,144,256]{2,1,0:T(8,128)(2,1)} broadcast(bf16[144,256]{1,0:T(8,128)(2,1)} %reduce_sum.39), dimensions={1,2} | broadcast | bytes 1253376 | tf_op jit(solution)/shard_map/broadcast_in_dim | solution.py:30
  39.9 3.7 %all-to-all-start.1 = ((bf16[16,144,256]{2,1,0:T(8,128)(2,1)}), bf16[16,144,256]{2,1,0:T(8,128)(2,1)S(1)}, u32[]{:S(2)}, u32[]{:S(2)}) async-start(bf16[16,144,256]{2,1,0:T(8,128)(2,1)} %broadcast_in_dim.4), calls=%async_computation.1 | async-start | bytes 2359296 | tf_op jit(solution)/shard_map/all_to_all | solution.py:29
  43.6 1.3 fusion.8
  44.9 14.6 %all-to-all-done.1 = bf16[16,144,256]{2,1,0:T(8,128)(2,1)S(1)} async-done(((bf16[16,144,256]{2,1,0:T(8,128)(2,1)}), bf16[16,144,256]{2,1,0:T(8,128)(2,1)S(1)}, u32[]{:S(2)}, u32[]{:S(2)}) %all-to-all-start.1) | async-done | bytes 1179680 | tf_op jit(solution)/shard_map/all_to_all | solution.py:29
  59.6 1.2 broadcast_in_dim.5
  60.8 21.0 %all-to-all-start.3 = ((f32[16,1,1]{2,1,0:T(1,128)}), f32[16,1,1]{2,1,0:T(1,128)}, u32[]{:S(2)}, u32[]{:S(2)}) async-start(f32[16,1,1]{2,1,0:T(1,128)} %broadcast_in_dim.5), calls=%async_computation.3 | async-start | bytes 16384 | tf_op jit(solution)/shard_map/all_to_all | solution.py:29
  81.9 6.7 %convolution_convert_fusion.2 = bf16[256,1792]{1,0:T(8,128)(2,1)} fusion(bf16[2304,1792]{1,0:T(8,128)(2,1)} %param.8, bf16[2304,256]{1,0:T(8,128)(2,1)S(1)} %bitcast.12, f32[2304]{0:T(1024)S(1)} %get-tuple-element.7), kind=kOutput, calls=%fused_computation.2 | convolution fusion | flops 2116157440 | bytes 10363904 | tf_op jit(solution)/shard_map/dot_general | solution.py:73
  88.6 0.0 copy-start.1
  88.6 0.0 copy-start.2
  88.6 0.3 all-to-all-done.3
  88.9 7.0 %all-to-all-start.2 = ((bf16[16,16,1792]{2,1,0:T(8,128)(2,1)}), bf16[16,16,1792]{2,1,0:T(8,128)(2,1)S(1)}, u32[]{:S(2)}, u32[]{:S(2)}) async-start(bf16[16,16,1792]{2,1,0:T(8,128)(2,1)} %bitcast.13), calls=%async_computation.2 | async-start | bytes 1835008 | tf_op jit(solution)/shard_map/all_to_all | solution.py:45
  96.0 1.3 reduce_sum.42
  98.0 23.3 %all-to-all-done.2 = bf16[16,16,1792]{2,1,0:T(8,128)(2,1)S(1)} async-done(((bf16[16,16,1792]{2,1,0:T(8,128)(2,1)}), bf16[16,16,1792]{2,1,0:T(8,128)(2,1)S(1)}, u32[]{:S(2)}, u32[]{:S(2)}) %all-to-all-start.2) | async-done | bytes 917536 | tf_op jit(solution)/shard_map/all_to_all | solution.py:45
  121.2 0.1 convert_reduce_fusion
  121.4 0.0 copy-done.1
  121.4 0.0 copy-done.2
  121.4 0.8 divide_convert_fusion
  122.2 17.0 %all_gather.11 = bf16[256,1792]{1,0:T(8,128)(2,1)S(1)} all-gather(bf16[16,1792]{1,0:T(8,128)(2,1)S(1)} %get-tuple-element.3), channel_id=1, replica_groups=mesh['dp'=16,'tensor'=16] {'dp'}, dimensions={0}, use_global_device_ids=true | all-gather | bytes 974848 | tf_op jit(solution)/shard_map/all_gather | solution.py:92
  139.1 0.0 all-gather.3.cloned.1.call-done
  139.1 2.8 %convolution_convert_fusion.1 = bf16[512,1792]{1,0:T(8,128)(2,1)} fusion(bf16[256,1792]{1,0:T(8,128)(2,1)S(1)} %all_gather.11, bf16[16,512,256]{2,1,0:T(8,128)(2,1)} %bitcast.15, s32[]{:T(128)S(6)} %select_n.10), kind=kOutput, calls=%fused_computation.1 | convolution fusion | flops 470679552 | bytes 3014660 | tf_op jit(solution)/shard_map/dot_general | solution.py:90
Async XLA Ops:
  7.2 1.7 %copy-start = (bf16[2304,512]{1,0:T(8,128)(2,1)S(1)}, bf16[2304,512]{1,0:T(8,128)(2,1)}, u32[]{:S(2)}) copy-start(bf16[2304,512]{1,0:T(8,128)(2,1)} %param.7) | copy-start | bytes 7077892
  7.2 132.0 %all-gather.3.cloned.1.call-start = ((), (), s32[]{:S(2)}) async-start(), calls=%async_computation.4 | async-start | bytes 4456448 | tf_op jit(solution)/shard_map/all_gather | solution.py:61
  39.9 19.7 %all-to-all-start.1 = ((bf16[16,144,256]{2,1,0:T(8,128)(2,1)}), bf16[16,144,256]{2,1,0:T(8,128)(2,1)S(1)}, u32[]{:S(2)}, u32[]{:S(2)}) async-start(bf16[16,144,256]{2,1,0:T(8,128)(2,1)} %broadcast_in_dim.4), calls=%async_computation.1 | async-start | bytes 2359296 | tf_op jit(solution)/shard_map/all_to_all | solution.py:29
  60.8 28.1 %all-to-all-start.3 = ((f32[16,1,1]{2,1,0:T(1,128)}), f32[16,1,1]{2,1,0:T(1,128)}, u32[]{:S(2)}, u32[]{:S(2)}) async-start(f32[16,1,1]{2,1,0:T(1,128)} %broadcast_in_dim.5), calls=%async_computation.3 | async-start | bytes 16384 | tf_op jit(solution)/shard_map/all_to_all | solution.py:29
  88.6 32.8 %copy-start.1 = (f32[16,1792]{1,0:T(8,128)S(1)}, f32[16,1792]{1,0:T(8,128)}, u32[]{:S(2)}) copy-start(f32[16,1792]{1,0:T(8,128)} %param.11) | copy-start | bytes 344068
  88.6 32.8 %copy-start.2 = (f32[16,1792]{1,0:T(8,128)S(1)}, f32[16,1792]{1,0:T(8,128)}, u32[]{:S(2)}) copy-start(f32[16,1792]{1,0:T(8,128)} %param.10) | copy-start | bytes 344068
  88.9 32.3 %all-to-all-start.2 = ((bf16[16,16,1792]{2,1,0:T(8,128)(2,1)}), bf16[16,16,1792]{2,1,0:T(8,128)(2,1)S(1)}, u32[]{:S(2)}, u32[]{:S(2)}) async-start(bf16[16,16,1792]{2,1,0:T(8,128)(2,1)} %bitcast.13), calls=%async_computation.2 | async-start | bytes 1835008 | tf_op jit(solution)/shard_map/all_to_all | solution.py:45
Sparse Core Ops, SparseCore 0:
  10.4 67.8 all-gather.2
where the time goes:
time: 149 us
  blocking collectives  43.5 us (29%)
  waiting for transfers between devices  38.9 us (26%)
  starting transfers between devices  31.8 us (21%)
  between operations  14.8 us (10%)
  matrix products  11.3 us (8%)
  other arithmetic  4.34 us (3%)
  local copies, waits for them, and re-layouts  4.16 us (3%)
    all_to_all x1, blocking collectives, sum_at_owner(): lax.all_to_all(parts, axis, split_axis=0, concat_axis=0, tiled=True)  26.5 us
    all_to_all x2, starting transfers between devices, sent_to_all(): lax.all_to_all(jnp.broadcast_to(shard[None], (size, *shard.shape)), axis,...  24.7 us
    all_to_all x1, waiting for transfers between devices, sum_at_owner(): lax.all_to_all(parts, axis, split_axis=0, concat_axis=0, tiled=True)  23.3 us
    all_gather x1, blocking collectives, local(): lax.all_gather(update, 'dp', axis=0, tiled=True)  17 us
    all_to_all x2, waiting for transfers between devices, sent_to_all(): lax.all_to_all(jnp.broadcast_to(shard[None], (size, *shard.shape)), axis,...  15 us
    all_to_all x1, starting transfers between devices, sum_at_owner(): lax.all_to_all(parts, axis, split_axis=0, concat_axis=0, tiled=True)  7.04 us
    dot_general x1, matrix products, local(): lax.dot_general(weighted, out_grads, (((0,), (0,)), ((), ())), preferred_...  6.72 us
    broadcast_in_dim x2, local copies, waits for them, and re-layouts, sent_to_all(): jnp.broadcast_to(shard[None], (size, *shard.shape))  3.22 us
  transfers between devices with their start and end apart: 4, of which 3 were waited for; matrix products, arithmetic and copies ran while one was open for 11% of the time, Pallas kernels for 0%

commit v1 on v0

v1 whole, which is shorter than its diff:
```python
import jax
import jax.numpy as jnp
from jax import lax
from jax.experimental import pallas as pl
from jax.experimental.pallas import tpu as pltpu
from jax.sharding import PartitionSpec as P

ADAM_STEP = 100
PAD = 128004
TEMP = 0.2
B1 = 0.9
B2 = 0.999
EPS = 1e-8
MESH = pl.DeviceIdType.MESH
F32 = jnp.float32
BF16 = jnp.bfloat16

NX = NY = 4
NZ = 8
TOK = 2304
HALF = TOK // 2
D = 512
R = 256
FF = 1792
ROWS = 16
BLK = R // NX
HB = BLK // 2
CUT = (0, 1024, FF)
WID = (1024, 768)
TOKENS = TOK * 16
SLOT = {4: 0, 3: 1, 5: 2, 2: 3, 6: 4, 1: 5, 7: 6, 0: 7}
PIECES = ((0, 3), (3, 2), (5, 3))


def rows(ref, start, size):
    return ref.at[pl.ds(pl.multiple_of(start, 16), size)]


def load(ref, start, size):
    return ref[pl.ds(pl.multiple_of(start, 16), size), :].astype(F32)


def kernel(
    act, og, basis, m1, m2, codes, ids, nf_o, ns_o, wu_o,
    act_v, og_v, basis_v, basis_t, m1_v, m2_v, codes_v, ids_v, wrow,
    px, py, wx, wy, r1, t1, s1, r2, raw,
    nsend, nrecv, cs0, cs1, cr0, cr1,
    tx0, tx1, rx0, rx1, u0, u1, own_v, nf_v, ns_v, wu_v,
    lsem, osem, xs, xr, nss, nrs, ces, cer, zs, zr, gs, gr, fs, fr, bs, br, bl,
):
    dp = lax.axis_index("dp")
    tn = lax.axis_index("tensor")
    z, c = dp // 2, dp % 2
    y, x = tn // NX, tn % NX

    def at(dx=0, dy=0, dz=0, dc=0):
        return (
            ((z + dz) % NZ) * 2 + (c + dc) % 2,
            ((y + dy) % NY) * NX + (x + dx) % NX,
        )

    partners = [at(dx=j) for j in (1, 2, 3)] + [at(dy=j) for j in (1, 2, 3)]
    partners += [at(dz=1), at(dz=NZ - 1), at(dc=1)]
    barrier = pltpu.get_barrier_semaphore()
    for other in partners:
        pl.semaphore_signal(barrier, inc=1, device_id=other, device_id_type=MESH)

    pending = []

    def send(src, dst, ssem, rsem, to):
        copy = pltpu.make_async_remote_copy(
            src_ref=src, dst_ref=dst, send_sem=ssem, recv_sem=rsem,
            device_id=to, device_id_type=MESH,
        )
        copy.start()
        pending.append(copy)
        return copy

    def fetch(src, dst, n):
        copy = pltpu.make_async_copy(src, dst, lsem.at[n])
        copy.start()
        return copy

    f_basis = fetch(basis, basis_v, 0)
    step = TOK // 6
    f_act = [
        fetch(act.at[pl.ds(i * step, step)], act_v.at[pl.ds(i * step, step)], 1 + i)
        for i in range(6)
    ]
    f_codes = fetch(codes, codes_v, 7)
    f_ids = fetch(ids, ids_v, 8)
    f_m1 = fetch(m1, m1_v, 9)
    f_m2 = fetch(m2, m2_v, 10)
    f_og = [
        fetch(og.at[pl.ds(i * HALF, HALF)], og_v.at[pl.ds(i * HALF, HALF)], 11 + i)
        for i in range(2)
    ]

    f_basis.wait()
    basis_t[...] = basis_v[...].T
    for i in range(6):
        f_act[i].wait()
        part = lax.dot_general(
            basis_t[...], act_v[i * step : (i + 1) * step, :],
            (((1,), (1,)), ((), ())), preferred_element_type=F32,
        ).astype(BF16)
        into = px if i < 3 else py
        into[:, (i % 3) * step : (i % 3 + 1) * step] = part

    pl.semaphore_wait(barrier, len(partners))

    class Unit:
        pass

    units = []
    for n, (p, w, pf, ps) in enumerate(((px, wx, x, y), (py, wy, y, x))):
        u = Unit()
        u.n, u.p, u.w, u.pf, u.ps = n, p, w, pf, ps
        u.first = (lambda j: at(dx=j % 4)) if n == 0 else (lambda j: at(dy=j % 4))
        u.second = (lambda j: at(dy=j % 4)) if n == 0 else (lambda j: at(dx=j % 4))
        u.r1, u.t1, u.s1, u.r2 = r1.at[n], t1.at[n], s1.at[n], r2.at[n]
        u.sem = lambda i, n=n: (xs.at[n, i], xr.at[n, i])
        units.append(u)

    def stage1(u):
        q2, qr, ql = (u.pf + 2) % 4, (u.pf + 1) % 4, (u.pf + 3) % 4
        u.a = [None] * 6
        u.a[0] = send(rows(u.p, q2 * BLK, HB), u.r1.at[0], *u.sem(0), u.first(1))
        u.a[3] = send(rows(u.p, q2 * BLK + HB, HB), u.r1.at[3], *u.sem(3), u.first(3))
        u.a[1] = send(rows(u.p, qr * BLK + HB, HB), u.r1.at[1], *u.sem(1), u.first(1))
        u.a[4] = send(rows(u.p, ql * BLK, HB), u.r1.at[4], *u.sem(4), u.first(3))

    def stage2(u):
        qr, ql = (u.pf + 1) % 4, (u.pf + 3) % 4
        u.a[0].wait_recv()
        u.t1[0] = (load(u.p, qr * BLK, HB) + u.r1[0].astype(F32)).astype(BF16)
        u.a[2] = send(u.t1.at[0], u.r1.at[2], *u.sem(2), u.first(1))
        u.a[3].wait_recv()
        u.t1[1] = (load(u.p, ql * BLK + HB, HB) + u.r1[3].astype(F32)).astype(BF16)
        u.a[5] = send(u.t1.at[1], u.r1.at[5], *u.sem(5), u.first(3))

    def stage3(u):
        for i in (1, 4, 2, 5):
            u.a[i].wait_recv()
        low = load(u.p, u.pf * BLK, HB) + u.r1[2].astype(F32) + u.r1[4].astype(F32)
        u.s1[0:HB, :] = low.astype(BF16)
        high = load(u.p, u.pf * BLK + HB, HB) + u.r1[1].astype(F32) + u.r1[5].astype(F32)
        u.s1[HB:BLK, :] = high.astype(BF16)
        u.b = [
            send(rows(u.s1, ((u.ps + j) % 4) * ROWS, ROWS), u.r2.at[j - 1], *u.sem(5 + j), u.second(j))
            for j in (1, 2, 3)
        ]

    def stage4(u):
        for copy in u.b:
            copy.wait_recv()
        total = load(u.s1, u.ps * ROWS, ROWS)
        for j in range(3):
            total = total + u.r2[j].astype(F32)
        total = total * wrow[:, u.n * HALF : (u.n + 1) * HALF]
        mine = u.pf * BLK + u.ps * ROWS
        u.w[pl.ds(pl.multiple_of(mine, 16), ROWS), :] = total.astype(BF16)
        u.c = [
            send(rows(u.w, mine, ROWS), rows(u.w, mine, ROWS), *u.sem(8 + j), u.second(j))
            for j in (1, 2, 3)
        ]

    def stage5(u):
        for copy in u.c:
            copy.wait_recv()
        low, high = rows(u.w, u.pf * BLK, HB), rows(u.w, u.pf * BLK + HB, HB)
        u.d = [None] * 6
        u.d[0] = send(low, low, *u.sem(12), u.first(1))
        u.d[3] = send(high, high, *u.sem(15), u.first(3))
        u.d[1] = send(high, high, *u.sem(13), u.first(1))
        u.d[4] = send(low, low, *u.sem(16), u.first(3))

    def stage6(u):
        u.d[0].wait_recv()
        low = rows(u.w, ((u.pf + 3) % 4) * BLK, HB)
        u.d[2] = send(low, low, *u.sem(14), u.first(1))
        u.d[3].wait_recv()
        high = rows(u.w, ((u.pf + 1) % 4) * BLK + HB, HB)
        u.d[5] = send(high, high, *u.sem(17), u.first(3))

    def stage7(u):
        for i in (1, 4, 2, 5):
            u.d[i].wait_recv()

    for u in units:
        stage1(u)

    f_codes.wait()
    f_ids.wait()
    weights = jnp.where(ids_v[...] == PAD, 0.0, jnp.exp(TEMP * codes_v[...].astype(F32)))
    for i in range(TOK // 128):
        wrow[:, i * 128 : (i + 1) * 128] = jnp.broadcast_to(weights[i : i + 1, :], (ROWS, 128))
    local = jnp.sum(jnp.sum(weights, axis=0, keepdims=True), axis=1, keepdims=True)
    nsend[0] = jnp.broadcast_to(local, (8, 128))
    ncore = send(nsend.at[0], nrecv.at[7], nss.at[7], nrs.at[7], at(dc=1))

    for u in units:
        stage2(u)
    ncore.wait_recv()
    nsend[1] = nsend[0] + nrecv[7]
    nr = send(nsend.at[1], nrecv.at[0], nss.at[0], nrs.at[0], at(dz=1))
    nl = send(nsend.at[1], nrecv.at[4], nss.at[4], nrs.at[4], at(dz=NZ - 1))
    for u in units:
        stage3(u)

    def norm_hop(i, nr, nl):
        nr.wait_recv()
        nr = send(nrecv.at[i - 1], nrecv.at[i], nss.at[i], nrs.at[i], at(dz=1))
        if i < 3:
            nl.wait_recv()
            nl = send(nrecv.at[3 + i], nrecv.at[4 + i], nss.at[4 + i], nrs.at[4 + i], at(dz=NZ - 1))
        return nr, nl

    nr, nl = norm_hop(1, nr, nl)
    for u in units:
        stage4(u)
    nr, nl = norm_hop(2, nr, nl)
    for u in units:
        stage5(u)
    nr, nl = norm_hop(3, nr, nl)
    for u in units:
        stage6(u)
    nr.wait_recv()
    nl.wait_recv()
    scale = nsend[1]
    for i in range(7):
        scale = scale + nrecv[i]
    scale = TOKENS / scale[0:1, 0:1]
    for copy in f_og:
        copy.wait()
    for u in units:
        stage7(u)

    x0, y0 = dp % NX, dp // NX
    in_row, in_col = y == y0, x == x0
    is_src = jnp.logical_and(in_row, in_col)
    parts = (pl.ds(0, D // 2), pl.ds(D // 2, D // 2))
    hop = ((lambda j: at(dx=j), lambda j: at(dy=j)), (lambda j: at(dy=j), lambda j: at(dx=j)))
    member = (in_row, in_col)

    def spread(h, level, src):
        copies = []
        for j in (1, 2, 3):
            i = h * 6 + level * 3 + j - 1
            copies.append(
                pltpu.make_async_remote_copy(
                    src_ref=src.at[parts[h]], dst_ref=own_v.at[parts[h]],
                    send_sem=bs.at[i], recv_sem=br.at[h],
                    device_id=hop[h][level](j), device_id_type=MESH,
                )
            )
        return copies

    def basis_first():
        @pl.when(is_src)
        def _():
            pltpu.make_async_copy(basis_v, own_v, bl).start()
            for h in (0, 1):
                for copy in spread(h, 0, basis_v):
                    copy.start()
            for h in (0, 1):
                for copy in spread(h, 1, basis_v):
                    copy.start()

    def basis_second():
        for h in (0, 1):
            @pl.when(jnp.logical_and(member[h], jnp.logical_not(is_src)))
            def _(h=h):
                copies = spread(h, 1, own_v)
                copies[0].wait_recv()
                for copy in copies:
                    copy.start()

    def basis_last():
        @pl.when(is_src)
        def _():
            pltpu.make_async_copy(basis_v, own_v, bl).wait()
            for h in (0, 1):
                for copy in spread(h, 0, basis_v):
                    copy.wait_send()

        for h in (0, 1):
            copies = spread(h, 1, own_v)

            @pl.when(jnp.logical_not(member[h]))
            def _(copies=copies):
                copies[0].wait_recv()

            @pl.when(member[h])
            def _(copies=copies):
                for copy in copies:
                    copy.wait_send()

    cs, cr, tx, rx, up = (cs0, cs1), (cr0, cr1), (tx0, tx1), (rx0, rx1), (u0, u1)
    exch = [[], []]

    def block_of(k, core):
        return (((z + k) % NZ) * 2 + core) * ROWS

    def raw_columns(h):
        for lo in range(CUT[h], CUT[h + 1], 256):
            raw[:, lo : lo + 256] = jnp.dot(
                wx[...], og_v[0:HALF, lo : lo + 256], preferred_element_type=F32
            ) + jnp.dot(wy[...], og_v[HALF:TOK, lo : lo + 256], preferred_element_type=F32)
        for n, (at_slot, count) in enumerate(PIECES):
            for k, slot in SLOT.items():
                if at_slot <= slot < at_slot + count:
                    cs[h][slot] = raw[
                        pl.ds(pl.multiple_of(block_of(k, 1 - c), 16), ROWS), CUT[h] : CUT[h + 1]
                    ].astype(BF16)
            span = pl.ds(at_slot, count)
            exch[h].append(
                send(cs[h].at[span], cr[h].at[span], ces.at[h, n], cer.at[h, n], at(dc=1))
            )

    def chip_sum(k, h):
        mine = raw[pl.ds(pl.multiple_of(block_of(k, c), 16), ROWS), CUT[h] : CUT[h + 1]]
        return mine + cr[h][SLOT[k]].astype(F32)

    arrived = {}

    def ring_send(h, way, s):
        length = 4 if way == h else 3
        if s > length:
            return
        k = (length + 1 - s) if way == 0 else (NZ - (length + 1 - s))
        total = chip_sum(k, h)
        if s > 1:
            arrived[h, way].wait_recv()
            total = total + rx[h][way * 4 + s - 2].astype(F32)
        i = way * 4 + s - 1
        tx[h][i] = total.astype(BF16)
        arrived[h, way] = send(
            tx[h].at[i], rx[h].at[i], zs.at[h, i], zr.at[h, i], at(dz=1 if way == 0 else NZ - 1)
        )

    basis_first()
    for h in (0, 1):
        raw_columns(h)
        exch[h][0].wait_recv()
        for way in (h, 1 - h):
            ring_send(h, way, 1)
    basis_second()
    for h in (0, 1):
        exch[h][1].wait_recv()
        exch[h][2].wait_recv()
    for s in (2, 3, 4):
        for h in (0, 1):
            for way in (h, 1 - h):
                ring_send(h, way, s)

    bias1 = 1.0 - B1**ADAM_STEP
    bias2 = 1.0 - B2**ADAM_STEP
    f_m1.wait()
    f_m2.wait()

    outs = []

    def store(src, dst, n):
        copy = pltpu.make_async_copy(src, dst, osem.at[n])
        copy.start()
        outs.append(copy)

    forwards = {}
    gathered = {}

    def gather_send(h, way, s):
        length = 4 if way == h else 3
        if s > length:
            return
        origin = (z + (NZ - (s - 1) if way == 0 else s - 1)) % NZ
        block = up[h].at[origin * 2 + c]
        i = way * 4 + s - 1
        gathered[h, way, s] = send(
            block, block, gs.at[h, i], gr.at[h, i], at(dz=1 if way == 0 else NZ - 1)
        )

    def forward(h, off):
        block = up[h].at[((z + off) % NZ) * 2 + c]
        forwards[h, off] = send(block, block, fs.at[h, off], fr.at[h, off], at(dc=1))

    for h in (0, 1):
        for way in (0, 1):
            arrived[h, way].wait_recv()
        last = (3 if h == 0 else 2, 4 + (3 if h == 1 else 2))
        grad = chip_sum(0, h) + rx[h][last[0]].astype(F32) + rx[h][last[1]].astype(F32)
        grad = grad * scale
        cols = slice(CUT[h], CUT[h + 1])
        first = B1 * m1_v[:, cols] + (1.0 - B1) * grad
        second = B2 * m2_v[:, cols] + (1.0 - B2) * grad * grad
        up[h][dp] = ((first / bias1) / (jnp.sqrt(second / bias2) + EPS)).astype(BF16)
        for way in (h, 1 - h):
            gather_send(h, way, 1)
        forward(h, 0)
        nf_v[:, cols] = first
        ns_v[:, cols] = second
    store(nf_v, nf_o, 0)
    store(ns_v, ns_o, 1)
    for s in (1, 2, 3, 4):
        for h in (0, 1):
            for way in (h, 1 - h):
                if (h, way, s) in gathered:
                    gathered[h, way, s].wait_recv()
                    gather_send(h, way, s + 1)
                    forward(h, (NZ - s) % NZ if way == 0 else s)
    basis_last()
    for h in (0, 1):
        for off in range(NZ):
            forwards[h, off].wait_recv()
        for lo in range(0, WID[h], 256):
            wu_v[:, CUT[h] + lo : CUT[h] + lo + 256] = jnp.dot(
                own_v[...], up[h][:, :, lo : lo + 256].reshape(R, 256), preferred_element_type=F32
            ).astype(BF16)
        cols = pl.ds(CUT[h], WID[h])
        store(wu_v.at[:, cols], wu_o.at[:, cols], 2 + h)
    for copy in pending:
        copy.wait_send()
    for copy in outs:
        copy.wait()


def local(activations, out_grads, basis, first_moment, second_moment, reward_codes, token_ids):
    any_ = pl.BlockSpec(memory_space=pl.ANY)
    vm = pltpu.VMEM
    dma = pltpu.SemaphoreType.DMA
    return pl.pallas_call(
        kernel,
        out_shape=(
            jax.ShapeDtypeStruct((ROWS, FF), F32),
            jax.ShapeDtypeStruct((ROWS, FF), F32),
            jax.ShapeDtypeStruct((D, FF), BF16),
        ),
        in_specs=[any_] * 7,
        out_specs=(any_, any_, any_),
        scratch_shapes=[
            vm((TOK, D), BF16), vm((TOK, FF), BF16), vm((D, R), BF16), vm((R, D), BF16),
            vm((ROWS, FF), F32), vm((ROWS, FF), F32),
            vm((TOK // 128, 128), jnp.int32), vm((TOK // 128, 128), jnp.int32),
            vm((ROWS, TOK), F32),
            vm((R, HALF), BF16), vm((R, HALF), BF16), vm((R, HALF), BF16), vm((R, HALF), BF16),
            vm((2, 6, HB, HALF), BF16), vm((2, 2, HB, HALF), BF16), vm((2, BLK, HALF), BF16),
            vm((2, 3, ROWS, HALF), BF16), vm((R, FF), F32),
            vm((2, 8, 128), F32), vm((8, 8, 128), F32),
            vm((8, ROWS, WID[0]), BF16), vm((8, ROWS, WID[1]), BF16),
            vm((8, ROWS, WID[0]), BF16), vm((8, ROWS, WID[1]), BF16),
            vm((8, ROWS, WID[0]), BF16), vm((8, ROWS, WID[1]), BF16),
            vm((8, ROWS, WID[0]), BF16), vm((8, ROWS, WID[1]), BF16),
            vm((16, ROWS, WID[0]), BF16), vm((16, ROWS, WID[1]), BF16),
            vm((D, R), BF16), vm((ROWS, FF), F32), vm((ROWS, FF), F32), vm((D, FF), BF16),
            dma((13,)), dma((4,)), dma((2, 18)), dma((2, 18)), dma((8,)), dma((8,)),
            dma((2, 3)), dma((2, 3)), dma((2, 8)), dma((2, 8)), dma((2, 8)), dma((2, 8)),
            dma((2, 8)), dma((2, 8)), dma((12,)), dma((2,)), dma,
        ],
        compiler_params=pltpu.CompilerParams(
            collective_id=0, has_side_effects=True, vmem_limit_bytes=48 * 1024 * 1024
        ),
        name="galore_step",
    )(
        activations, out_grads, basis, first_moment, second_moment,
        reward_codes.reshape(TOK // 128, 128), token_ids.reshape(TOK // 128, 128),
    )


def solution(mesh):
    return jax.shard_map(
        local,
        mesh=mesh,
        in_specs=(
            P("dp", "tensor"),
            P("dp", "tensor"),
            P("tensor", None),
            P("dp", "tensor"),
            P("dp", "tensor"),
            P("dp"),
            P("dp"),
        ),
        out_specs=(P("dp", "tensor"), P("dp", "tensor"), P("dp", "tensor")),
        check_vma=False,
    )
```

time: 149 us -> 79 us (0.53)
  Pallas kernels: 0 us -> 69.7 us
  blocking collectives: 43.5 us -> 0 us
  waiting for transfers between devices: 38.9 us -> 0 us
  starting transfers between devices: 31.8 us -> 0 us
  between operations: 14.8 us -> 0.66 us
  matrix products: 11.3 us -> 0 us
  other arithmetic: 4.34 us -> 0 us
  local copies, waits for them, and re-layouts: 4.16 us -> 8.34 us
    pallas_call x0 -> x1, Pallas kernels: none -> 69.7 us  [local(): pl.pallas_call(kernel, out_shape=(jax.ShapeDtypeStruct((ROWS, FF), F32),...]
    all_to_all x3 -> x0, waiting for transfers between devices: 38.2 us -> none  [the longest x1 23.3 us: sum_at_owner(): lax.all_to_all(parts, axis, split_axis=0, concat_axis=0, tiled=True)]
    all_to_all x3 -> x0, starting transfers between devices: 31.8 us -> none  [the longest x2 24.7 us: sent_to_all(): lax.all_to_all(jnp.broadcast_to(shard[None], (size, *shard.shape)), axis,...]
    all_to_all x1 -> x0, blocking collectives: 26.5 us -> none  [sum_at_owner(): lax.all_to_all(parts, axis, split_axis=0, concat_axis=0, tiled=True)]
    all_gather x1 -> x0, blocking collectives: 17 us -> none  [local(): lax.all_gather(update, 'dp', axis=0, tiled=True)]
    dot_general x3 -> x0, matrix products: 11.3 us -> none  [the longest x1 6.72 us: local(): lax.dot_general(weighted, out_grads, (((0,), (0,)), ((), ())), preferred_...]
    unnamed x6 -> x15, local copies, waits for them, and re-layouts: 0.94 us -> 8.34 us
    reduce_sum x4 -> x0, other arithmetic: 3.58 us -> none  [the longest x1 1.34 us: local(): local_total = jnp.sum(weights)]
  transfers between devices with their start and end apart: 4 -> 0, of which waited for: 3 -> 0; matrix products, arithmetic and copies ran while one was open for 11% -> 0% of each run, Pallas kernels for 0% -> 0%
where the time goes in v1:
time: 79 us; the launch traced here: 78.7 us
  Pallas kernels  69.7 us (88%)
  local copies, waits for them, and re-layouts  8.34 us (11%)
    pallas_call x1, Pallas kernels, local(): pl.pallas_call(kernel, out_shape=(jax.ShapeDtypeStruct((ROWS, FF), F32),...  69.7 us
    unnamed x15, local copies, waits for them, and re-layouts  8.34 us

profile of v1, /device:TPU:1, one launch (start us, length us, event | category | flops | bytes accessed | tf_op | source)
XLA Modules:
  0.0 78.7 jit_solution(4700503130025627948)
XLA Ops:
  0.6 0.0 copy-start
  0.6 1.7 %copy-done = bf16[2304,512]{1,0:T(8,128)(2,1)S(1)} copy-done((bf16[2304,512]{1,0:T(8,128)(2,1)S(1)}, bf16[2304,512]{1,0:T(8,128)(2,1)}, u32[]{:S(2)}) %copy-start) | copy-done | bytes 2359320
  2.3 0.0 copy-start.1
  2.3 0.9 %copy-done.1 = bf16[512,256]{1,0:T(8,128)(2,1)S(1)} copy-done((bf16[512,256]{1,0:T(8,128)(2,1)S(1)}, bf16[512,256]{1,0:T(8,128)(2,1)}, u32[]{:S(2)}) %copy-start.1) | copy-done | bytes 262168
  3.2 0.0 copy-start.2
  3.3 0.9 %copy-done.2 = f32[16,1792]{1,0:T(8,128)S(1)} copy-done((f32[16,1792]{1,0:T(8,128)S(1)}, f32[16,1792]{1,0:T(8,128)}, u32[]{:S(2)}) %copy-start.2) | copy-done | bytes 114712
  4.1 0.0 copy-start.3
  4.2 0.9 %copy-done.3 = f32[16,1792]{1,0:T(8,128)S(1)} copy-done((f32[16,1792]{1,0:T(8,128)S(1)}, f32[16,1792]{1,0:T(8,128)}, u32[]{:S(2)}) %copy-start.3) | copy-done | bytes 114712
  5.0 0.0 copy-start.4
  5.0 0.7 copy-done.4
  5.8 0.0 copy-start.5
  5.8 0.7 copy-done.5
  6.5 69.7 %galore_step.1 = (f32[16,1792]{1,0:T(8,128)S(1)}, f32[16,1792]{1,0:T(8,128)S(1)}, bf16[512,1792]{1,0:T(8,128)(2,1)S(1)}) custom-call(bf16[2304,512]{1,0:T(8,128)(2,1)S(1)} %copy-done, bf16[2304,1792]{1,0:T(8,128)(2,1)} %og.1, bf16[512,256]{1,0:T(8,128)(2,1)S(1)} %copy-done.1, f32[16,1792]{1,0:T(8,128)S(1)} %copy-done.2, f32[16,1792]{1,0:T(8,128)S(1)} %copy-done.3, ...), custom_call_target="tpu_custom_call" | custom-call | tf_op jit(solution)/shard_map/galore_step/pallas_call | solution.py:431
  76.2 0.6 copy.13
  76.8 0.6 copy.14
  77.5 1.2 %copy.15 = bf16[512,1792]{1,0:T(8,128)(2,1)} copy(bf16[512,1792]{1,0:T(8,128)(2,1)S(1)} %get-tuple-element.8) | data formatting | bytes 3670016
Async XLA Ops:
  0.6 1.7 %copy-start = (bf16[2304,512]{1,0:T(8,128)(2,1)S(1)}, bf16[2304,512]{1,0:T(8,128)(2,1)}, u32[]{:S(2)}) copy-start(bf16[2304,512]{1,0:T(8,128)(2,1)} %act.1) | copy-start | bytes 7077892
  2.3 0.9 %copy-start.1 = (bf16[512,256]{1,0:T(8,128)(2,1)S(1)}, bf16[512,256]{1,0:T(8,128)(2,1)}, u32[]{:S(2)}) copy-start(bf16[512,256]{1,0:T(8,128)(2,1)} %basis.1) | copy-start | bytes 786436
  3.2 0.9 %copy-start.2 = (f32[16,1792]{1,0:T(8,128)S(1)}, f32[16,1792]{1,0:T(8,128)}, u32[]{:S(2)}) copy-start(f32[16,1792]{1,0:T(8,128)} %m1.1) | copy-start | bytes 344068
  4.1 0.9 %copy-start.3 = (f32[16,1792]{1,0:T(8,128)S(1)}, f32[16,1792]{1,0:T(8,128)}, u32[]{:S(2)}) copy-start(f32[16,1792]{1,0:T(8,128)} %m2.1) | copy-start | bytes 344068
  5.0 0.7 copy-start.4
  5.8 0.7 copy-start.5

commit v2 on v1

--- a/solution.py
+++ b/solution.py
@@ -41,12 +41,12 @@
 
 
 def kernel(
-    act, og, basis, m1, m2, codes, ids, nf_o, ns_o, wu_o,
+    act, og, basis, m1, m2, codes, ids, nf_v, ns_v, own_v, u0, u1,
     act_v, og_v, basis_v, basis_t, m1_v, m2_v, codes_v, ids_v, wrow,
     px, py, wx, wy, r1, t1, s1, r2, raw,
     nsend, nrecv, cs0, cs1, cr0, cr1,
-    tx0, tx1, rx0, rx1, u0, u1, own_v, nf_v, ns_v, wu_v,
-    lsem, osem, xs, xr, nss, nrs, ces, cer, zs, zr, gs, gr, fs, fr, bs, br, bl,
+    tx0, tx1, rx0, rx1,
+    lsem, xs, xr, nss, nrs, ces, cer, zs, zr, gs, gr, fs, fr, bs, br, bl,
 ):
     dp = lax.axis_index("dp")
     tn = lax.axis_index("tensor")
@@ -60,7 +60,7 @@
         )
 
     partners = [at(dx=j) for j in (1, 2, 3)] + [at(dy=j) for j in (1, 2, 3)]
-    partners += [at(dz=1), at(dz=NZ - 1), at(dc=1)]
+    partners += [at(dz=j) for j in range(1, NZ)] + [at(dc=1)]
     barrier = pltpu.get_barrier_semaphore()
     for other in partners:
         pl.semaphore_signal(barrier, inc=1, device_id=other, device_id_type=MESH)
@@ -203,30 +203,21 @@
         stage2(u)
     ncore.wait_recv()
     nsend[1] = nsend[0] + nrecv[7]
-    nr = send(nsend.at[1], nrecv.at[0], nss.at[0], nrs.at[0], at(dz=1))
-    nl = send(nsend.at[1], nrecv.at[4], nss.at[4], nrs.at[4], at(dz=NZ - 1))
+    sums = [
+        send(nsend.at[1], nrecv.at[j - 1], nss.at[j - 1], nrs.at[j - 1], at(dz=j))
+        for j in range(1, NZ)
+    ]
     for u in units:
         stage3(u)
 
-    def norm_hop(i, nr, nl):
-        nr.wait_recv()
-        nr = send(nrecv.at[i - 1], nrecv.at[i], nss.at[i], nrs.at[i], at(dz=1))
-        if i < 3:
-            nl.wait_recv()
-            nl = send(nrecv.at[3 + i], nrecv.at[4 + i], nss.at[4 + i], nrs.at[4 + i], at(dz=NZ - 1))
-        return nr, nl
-
-    nr, nl = norm_hop(1, nr, nl)
     for u in units:
         stage4(u)
-    nr, nl = norm_hop(2, nr, nl)
     for u in units:
         stage5(u)
-    nr, nl = norm_hop(3, nr, nl)
     for u in units:
         stage6(u)
-    nr.wait_recv()
-    nl.wait_recv()
+    for copy in sums:
+        copy.wait_recv()
     scale = nsend[1]
     for i in range(7):
         scale = scale + nrecv[i]
@@ -322,121 +313,105 @@
         mine = raw[pl.ds(pl.multiple_of(block_of(k, c), 16), ROWS), CUT[h] : CUT[h + 1]]
         return mine + cr[h][SLOT[k]].astype(F32)
 
-    arrived = {}
-
-    def ring_send(h, way, s):
-        length = 4 if way == h else 3
-        if s > length:
-            return
-        k = (length + 1 - s) if way == 0 else (NZ - (length + 1 - s))
-        total = chip_sum(k, h)
-        if s > 1:
-            arrived[h, way].wait_recv()
-            total = total + rx[h][way * 4 + s - 2].astype(F32)
-        i = way * 4 + s - 1
-        tx[h][i] = total.astype(BF16)
-        arrived[h, way] = send(
-            tx[h].at[i], rx[h].at[i], zs.at[h, i], zr.at[h, i], at(dz=1 if way == 0 else NZ - 1)
-        )
+    reduced = [[], []]
+
+    def reduce_sends(h, offsets):
+        for k in offsets:
+            tx[h][k - 1] = chip_sum(k, h).astype(BF16)
+            reduced[h].append(
+                send(tx[h].at[k - 1], rx[h].at[k - 1], zs.at[h, k - 1], zr.at[h, k - 1], at(dz=k))
+            )
 
     basis_first()
     for h in (0, 1):
         raw_columns(h)
         exch[h][0].wait_recv()
-        for way in (h, 1 - h):
-            ring_send(h, way, 1)
+        reduce_sends(h, (4, 3, 5))
+        exch[h][1].wait_recv()
+        reduce_sends(h, (2, 6))
+        exch[h][2].wait_recv()
+        reduce_sends(h, (1, 7))
     basis_second()
-    for h in (0, 1):
-        exch[h][1].wait_recv()
-        exch[h][2].wait_recv()
-    for s in (2, 3, 4):
-        for h in (0, 1):
-            for way in (h, 1 - h):
-                ring_send(h, way, s)
 
     bias1 = 1.0 - B1**ADAM_STEP
     bias2 = 1.0 - B2**ADAM_STEP
     f_m1.wait()
     f_m2.wait()
 
-    outs = []
-
-    def store(src, dst, n):
-        copy = pltpu.make_async_copy(src, dst, osem.at[n])
-        copy.start()
-        outs.append(copy)
-
-    forwards = {}
-    gathered = {}
-
-    def gather_send(h, way, s):
-        length = 4 if way == h else 3
-        if s > length:
-            return
-        origin = (z + (NZ - (s - 1) if way == 0 else s - 1)) % NZ
-        block = up[h].at[origin * 2 + c]
-        i = way * 4 + s - 1
-        gathered[h, way, s] = send(
-            block, block, gs.at[h, i], gr.at[h, i], at(dz=1 if way == 0 else NZ - 1)
-        )
+    forwards, gathered = {}, {}
 
     def forward(h, off):
         block = up[h].at[((z + off) % NZ) * 2 + c]
         forwards[h, off] = send(block, block, fs.at[h, off], fr.at[h, off], at(dc=1))
 
     for h in (0, 1):
-        for way in (0, 1):
-            arrived[h, way].wait_recv()
-        last = (3 if h == 0 else 2, 4 + (3 if h == 1 else 2))
-        grad = chip_sum(0, h) + rx[h][last[0]].astype(F32) + rx[h][last[1]].astype(F32)
+        for copy in reduced[h]:
+            copy.wait_recv()
+        grad = chip_sum(0, h)
+        for k in range(NZ - 1):
+            grad = grad + rx[h][k].astype(F32)
         grad = grad * scale
         cols = slice(CUT[h], CUT[h + 1])
         first = B1 * m1_v[:, cols] + (1.0 - B1) * grad
         second = B2 * m2_v[:, cols] + (1.0 - B2) * grad * grad
         up[h][dp] = ((first / bias1) / (jnp.sqrt(second / bias2) + EPS)).astype(BF16)
-        for way in (h, 1 - h):
-            gather_send(h, way, 1)
+        for k in (4, 3, 5, 2, 6, 1, 7):
+            gathered[h, k] = send(
+                up[h].at[dp], up[h].at[dp], gs.at[h, k], gr.at[h, k], at(dz=k)
+            )
         forward(h, 0)
         nf_v[:, cols] = first
         ns_v[:, cols] = second
-    store(nf_v, nf_o, 0)
-    store(ns_v, ns_o, 1)
-    for s in (1, 2, 3, 4):
-        for h in (0, 1):
-            for way in (h, 1 - h):
-                if (h, way, s) in gathered:
-                    gathered[h, way, s].wait_recv()
-                    gather_send(h, way, s + 1)
-                    forward(h, (NZ - s) % NZ if way == 0 else s)
+    for h in (0, 1):
+        for k in (1, 7, 2, 6, 3, 5, 4):
+            gathered[h, k].wait_recv()
+            forward(h, NZ - k)
     basis_last()
     for h in (0, 1):
         for off in range(NZ):
             forwards[h, off].wait_recv()
-        for lo in range(0, WID[h], 256):
-            wu_v[:, CUT[h] + lo : CUT[h] + lo + 256] = jnp.dot(
-                own_v[...], up[h][:, :, lo : lo + 256].reshape(R, 256), preferred_element_type=F32
-            ).astype(BF16)
-        cols = pl.ds(CUT[h], WID[h])
-        store(wu_v.at[:, cols], wu_o.at[:, cols], 2 + h)
     for copy in pending:
         copy.wait_send()
-    for copy in outs:
+
+
+def final_kernel(nf_v, ns_v, own_v, u0, u1, nf_o, ns_o, wu_o, wu_v, osem):
+    copies = [
+        pltpu.make_async_copy(nf_v, nf_o, osem.at[0]),
+        pltpu.make_async_copy(ns_v, ns_o, osem.at[1]),
+    ]
+    for copy in copies:
+        copy.start()
+    n = 2
+    for h, u in enumerate((u0, u1)):
+        for lo in range(0, WID[h], 256):
+            cols = pl.ds(CUT[h] + lo, 256)
+            wu_v[:, CUT[h] + lo : CUT[h] + lo + 256] = jnp.dot(
+                own_v[...], u[:, :, lo : lo + 256].reshape(R, 256), preferred_element_type=F32
+            ).astype(BF16)
+            copies.append(pltpu.make_async_copy(wu_v.at[:, cols], wu_o.at[:, cols], osem.at[n]))
+            copies[-1].start()
+            n += 1
+    for copy in copies:
         copy.wait()
 
 
 def local(activations, out_grads, basis, first_moment, second_moment, reward_codes, token_ids):
-    any_ = pl.BlockSpec(memory_space=pl.ANY)
+    hbm = pl.BlockSpec(memory_space=pltpu.HBM)
+    near = pl.BlockSpec(memory_space=pltpu.VMEM)
     vm = pltpu.VMEM
     dma = pltpu.SemaphoreType.DMA
-    return pl.pallas_call(
+    moments = jax.ShapeDtypeStruct((ROWS, FF), F32)
+    states = pl.pallas_call(
         kernel,
         out_shape=(
-            jax.ShapeDtypeStruct((ROWS, FF), F32),
-            jax.ShapeDtypeStruct((ROWS, FF), F32),
-            jax.ShapeDtypeStruct((D, FF), BF16),
+            vm((ROWS, FF), F32),
+            vm((ROWS, FF), F32),
+            vm((D, R), BF16),
+            vm((16, ROWS, WID[0]), BF16),
+            vm((16, ROWS, WID[1]), BF16),
         ),
-        in_specs=[any_] * 7,
-        out_specs=(any_, any_, any_),
+        in_specs=[hbm] * 7,
+        out_specs=(near,) * 5,
         scratch_shapes=[
             vm((TOK, D), BF16), vm((TOK, FF), BF16), vm((D, R), BF16), vm((R, D), BF16),
             vm((ROWS, FF), F32), vm((ROWS, FF), F32),
@@ -450,20 +425,27 @@
             vm((8, ROWS, WID[0]), BF16), vm((8, ROWS, WID[1]), BF16),
             vm((8, ROWS, WID[0]), BF16), vm((8, ROWS, WID[1]), BF16),
             vm((8, ROWS, WID[0]), BF16), vm((8, ROWS, WID[1]), BF16),
-            vm((16, ROWS, WID[0]), BF16), vm((16, ROWS, WID[1]), BF16),
-            vm((D, R), BF16), vm((ROWS, FF), F32), vm((ROWS, FF), F32), vm((D, FF), BF16),
-            dma((13,)), dma((4,)), dma((2, 18)), dma((2, 18)), dma((8,)), dma((8,)),
+            dma((13,)), dma((2, 18)), dma((2, 18)), dma((8,)), dma((8,)),
             dma((2, 3)), dma((2, 3)), dma((2, 8)), dma((2, 8)), dma((2, 8)), dma((2, 8)),
             dma((2, 8)), dma((2, 8)), dma((12,)), dma((2,)), dma,
         ],
         compiler_params=pltpu.CompilerParams(
-            collective_id=0, has_side_effects=True, vmem_limit_bytes=48 * 1024 * 1024
+            collective_id=0, has_side_effects=True, vmem_limit_bytes=55_260_000
         ),
         name="galore_step",
     )(
         activations, out_grads, basis, first_moment, second_moment,
         reward_codes.reshape(TOK // 128, 128), token_ids.reshape(TOK // 128, 128),
     )
+    return pl.pallas_call(
+        final_kernel,
+        out_shape=(moments, moments, jax.ShapeDtypeStruct((D, FF), BF16)),
+        in_specs=[near] * 5,
+        out_specs=(hbm, hbm, hbm),
+        scratch_shapes=[vm((D, FF), BF16), dma((9,))],
+        compiler_params=pltpu.CompilerParams(vmem_limit_bytes=16 * 1024 * 1024),
+        name="project_back",
+    )(*states)
 
 
 def solution(mesh):

time: 79 us -> 66.5 us (0.84)
  local copies, waits for them, and re-layouts: 8.34 us -> 0 us
  Pallas kernels: 69.7 us -> 65.7 us
    unnamed x15 -> x0, local copies, waits for them, and re-layouts: 8.34 us -> none
    pallas_call x1 -> x2, Pallas kernels: 69.7 us -> 65.7 us  [the longest x1 64.1 us: local(): pl.pallas_call(kernel, out_shape=(vm((ROWS, FF), F32), vm((ROWS, FF), F32...]
where the time goes in v2:
time: 66.5 us; the launch traced here: 66.4 us
  Pallas kernels  65.7 us (99%)
    pallas_call x1, Pallas kernels, local(): pl.pallas_call(kernel, out_shape=(vm((ROWS, FF), F32), vm((ROWS, FF), F32...  64.1 us
    pallas_call x1, Pallas kernels, local(): pl.pallas_call(final_kernel, out_shape=(moments, moments, jax.ShapeDtypeS...  1.59 us

profile of v2, /device:TPU:1, one launch (start us, length us, event | category | flops | bytes accessed | tf_op | source)
XLA Modules:
  0.0 66.4 jit_solution(12929388611506399161)
XLA Ops:
  0.6 64.1 %galore_step.1 = (f32[16,1792]{1,0:T(8,128)S(1)}, f32[16,1792]{1,0:T(8,128)S(1)}, bf16[512,256]{1,0:T(8,128)(2,1)S(1)}, bf16[16,16,1024]{2,1,0:T(8,128)(2,1)S(1)}, bf16[16,16,768]{2,1,0:T(8,128)(2,1)S(1)}) custom-call(bf16[2304,512]{1,0:T(8,128)(2,1)} %act.1, bf16[2304,1792]{1,0:T(8,128)(2,1)} %og.1, bf16[512,256]{1,0:T(8,128)(2,1)} %basis.1, ...), custom_call_target="tpu_custom_call" | custom-call | tf_op jit(solution)/shard_map/galore_step/pallas_call | solution.py:404
  64.8 1.6 %project_back.1 = (f32[16,1792]{1,0:T(8,128)}, f32[16,1792]{1,0:T(8,128)}, bf16[512,1792]{1,0:T(8,128)(2,1)}) custom-call(f32[16,1792]{1,0:T(8,128)S(1)} %get-tuple-element.8.nf_v, f32[16,1792]{1,0:T(8,128)S(1)} %get-tuple-element.9.ns_v, bf16[512,256]{1,0:T(8,128)(2,1)S(1)} %get-tuple-element.10.own_v, bf16[16,16,1024]{2,1,0:T(8,128)(2,1)S(1)} %get-tuple-element.11.u0, ...), custom_call_target="tpu_custom_call" | custom-call | tf_op jit(solution)/shard_map/project_back/pallas_call | solution.py:440

commit v3 on v2

v3 whole, which is shorter than its diff:
```python
import jax
import jax.numpy as jnp
from jax import lax
from jax.experimental import pallas as pl
from jax.experimental.pallas import tpu as pltpu
from jax.sharding import PartitionSpec as P

ADAM_STEP = 100
PAD = 128004
TEMP = 0.2
B1 = 0.9
B2 = 0.999
EPS = 1e-8
MESH = pl.DeviceIdType.MESH
F32 = jnp.float32
BF16 = jnp.bfloat16

NX = NY = 4
NZ = 8
TOK = 2304
HALF = TOK // 2
D = 512
R = 256
FF = 1792
ROWS = 16
PARTS = 2
RP = R // PARTS
BLK = RP // NX
SIDE = FF // 2
TOKENS = TOK * 16
SLOT = {4: 0, 3: 1, 5: 2, 2: 3, 6: 4, 1: 5, 7: 6, 0: 7}
PIECES = ((0, 3), (3, 2), (5, 3))


def rows(ref, start, size):
    return ref.at[pl.ds(pl.multiple_of(start, 16), size)]


def load(ref, start, size):
    return ref[pl.ds(pl.multiple_of(start, 16), size), :].astype(F32)


def side_by_side(ref, n):
    top = pl.ds(n * 8, 8)
    return jnp.concatenate([ref[top, 0:SIDE], ref[top, SIDE:FF]], axis=0)


def kernel(
    act, og, basis, m1, m2, codes, ids, nf_v, ns_v, own_v, up,
    act_v, og_v, basis_v, basis_t, m1_v, m2_v, codes_v, ids_v, wrow,
    p, w, r1, s1, r2, raw, nsend, nrecv, cs, cr, tx, rx,
    lsem, xs, xr, nss, nrs, ces, cer, zs, zr, gs, gr, fs, fr, bs, br, bl,
):
    dp = lax.axis_index("dp")
    tn = lax.axis_index("tensor")
    z, c = dp // 2, dp % 2
    y, x = tn // NX, tn % NX

    def at(dx=0, dy=0, dz=0, dc=0):
        return (
            ((z + dz) % NZ) * 2 + (c + dc) % 2,
            ((y + dy) % NY) * NX + (x + dx) % NX,
        )

    partners = [at(dx=j) for j in (1, 2, 3)] + [at(dy=j) for j in (1, 2, 3)]
    partners += [at(dz=j) for j in range(1, NZ)] + [at(dc=1)]
    barrier = pltpu.get_barrier_semaphore()
    for other in partners:
        pl.semaphore_signal(barrier, inc=1, device_id=other, device_id_type=MESH)

    pending = []

    def send(src, dst, ssem, rsem, to):
        copy = pltpu.make_async_remote_copy(
            src_ref=src, dst_ref=dst, send_sem=ssem, recv_sem=rsem,
            device_id=to, device_id_type=MESH,
        )
        copy.start()
        pending.append(copy)
        return copy

    def fetch(src, dst, n):
        copy = pltpu.make_async_copy(src, dst, lsem.at[n])
        copy.start()
        return copy

    f_basis = fetch(basis, basis_v, 0)
    step = TOK // 6
    f_act = [
        fetch(act.at[pl.ds(i * step, step)], act_v.at[pl.ds(i * step, step)], 1 + i)
        for i in range(6)
    ]
    f_codes = fetch(codes, codes_v, 7)
    f_ids = fetch(ids, ids_v, 8)
    f_m1 = fetch(m1, m1_v, 9)
    f_m2 = fetch(m2, m2_v, 10)
    f_og = [
        fetch(og.at[pl.ds(i * HALF, HALF)], og_v.at[pl.ds(i * HALF, HALF)], 11 + i)
        for i in range(2)
    ]

    f_basis.wait()
    turned = basis_v[...].astype(F32).T.reshape(16, PARTS, 8, D)
    for n in range(PARTS):
        basis_t[n * RP : (n + 1) * RP, :] = turned[:, n].reshape(RP, D).astype(BF16)
    for i in range(6):
        f_act[i].wait()
        part = lax.dot_general(
            basis_t[...], act_v[i * step : (i + 1) * step, :],
            (((1,), (1,)), ((), ())), preferred_element_type=F32,
        ).astype(BF16)
        for n in range(PARTS):
            p[n, :, i * step : (i + 1) * step] = part[n * RP : (n + 1) * RP, :]

    pl.semaphore_wait(barrier, len(partners))

    class Unit:
        pass

    units = []
    along_x, along_y = (lambda j: at(dx=j)), (lambda j: at(dy=j))
    for n in range(2 * PARTS):
        u = Unit()
        u.cols = pl.ds((n % 2) * HALF, HALF)
        u.n, u.p, u.w = n, p.at[n // 2, :, u.cols], w.at[n // 2, :, u.cols]
        u.pf = x if n % 2 == 0 else y
        u.first, u.second = (along_x, along_y) if n % 2 == 0 else (along_y, along_x)
        u.r1, u.s1, u.r2 = r1.at[n], s1.at[n], r2.at[n]
        units.append(u)

    def scatter_start(u):
        u.a = [
            send(rows(u.p, ((u.pf + j) % 4) * BLK, BLK), u.r1.at[j - 1],
                 xs.at[u.n, j - 1], xr.at[u.n, j - 1], u.first(j))
            for j in (2, 1, 3)
        ]

    def exchange_start(u):
        total = load(u.p, u.pf * BLK, BLK)
        for copy in u.a:
            copy.wait_recv()
        for j in range(3):
            total = total + u.r1[j].astype(F32)
        u.s1[...] = total.astype(BF16)
        u.b = [
            send(u.s1, u.r2.at[j - 1], xs.at[u.n, 2 + j], xr.at[u.n, 2 + j], u.second(j))
            for j in (2, 1, 3)
        ]

    def gather_start(u):
        for copy in u.b:
            copy.wait_recv()
        mine = pl.ds(pl.multiple_of(u.pf * BLK, 16), BLK)
        for lo in range(0, BLK, ROWS):
            total = u.s1[lo : lo + ROWS, :].astype(F32)
            for j in range(3):
                total = total + u.r2[j, lo : lo + ROWS, :].astype(F32)
            total = total * wrow[:, u.cols]
            u.w[pl.ds(pl.multiple_of(u.pf * BLK + lo, 16), ROWS), :] = total.astype(BF16)
        u.c = [
            send(u.w.at[mine], u.w.at[mine], xs.at[u.n, 5 + j], xr.at[u.n, 5 + j], u.first(j))
            for j in (2, 1, 3)
        ]

    def gather_end(u):
        for copy in u.c:
            copy.wait_recv()

    def units_of(n):
        return units[2 * n : 2 * n + 2]

    for u in units:
        scatter_start(u)

    f_codes.wait()
    f_ids.wait()
    weights = jnp.where(ids_v[...] == PAD, 0.0, jnp.exp(TEMP * codes_v[...].astype(F32)))
    for i in range(TOK // 128):
        wrow[:, i * 128 : (i + 1) * 128] = jnp.broadcast_to(weights[i : i + 1, :], (ROWS, 128))
    local = jnp.sum(jnp.sum(weights, axis=0, keepdims=True), axis=1, keepdims=True)
    nsend[0] = jnp.broadcast_to(local, (8, 128))
    ncore = send(nsend.at[0], nrecv.at[7], nss.at[7], nrs.at[7], at(dc=1))

    for u in units_of(0):
        exchange_start(u)
    ncore.wait_recv()
    nsend[1] = nsend[0] + nrecv[7]
    sums = [
        send(nsend.at[1], nrecv.at[j - 1], nss.at[j - 1], nrs.at[j - 1], at(dz=j))
        for j in range(1, NZ)
    ]
    for u in units_of(1):
        exchange_start(u)
    for n in range(PARTS):
        for u in units_of(n):
            gather_start(u)
    for copy in sums:
        copy.wait_recv()
    scale = nsend[1]
    for i in range(7):
        scale = scale + nrecv[i]
    scale = TOKENS / scale[0:1, 0:1]
    for copy in f_og + [f_m1, f_m2]:
        copy.wait()

    x0, y0 = dp % NX, dp // NX
    in_row, in_col = y == y0, x == x0
    is_src = jnp.logical_and(in_row, in_col)
    parts = (pl.ds(0, D // 2), pl.ds(D // 2, D // 2))
    hop = ((lambda j: at(dx=j), lambda j: at(dy=j)), (lambda j: at(dy=j), lambda j: at(dx=j)))
    member = (in_row, in_col)

    def spread(h, level, src):
        copies = []
        for j in (1, 2, 3):
            i = h * 6 + level * 3 + j - 1
            copies.append(
                pltpu.make_async_remote_copy(
                    src_ref=src.at[parts[h]], dst_ref=own_v.at[parts[h]],
                    send_sem=bs.at[i], recv_sem=br.at[h],
                    device_id=hop[h][level](j), device_id_type=MESH,
                )
            )
        return copies

    def basis_first():
        @pl.when(is_src)
        def _():
            pltpu.make_async_copy(basis_v, own_v, bl).start()
            for h in (0, 1):
                for copy in spread(h, 0, basis_v):
                    copy.start()
            for h in (0, 1):
                for copy in spread(h, 1, basis_v):
                    copy.start()

    def basis_second():
        for h in (0, 1):
            @pl.when(jnp.logical_and(member[h], jnp.logical_not(is_src)))
            def _(h=h):
                copies = spread(h, 1, own_v)
                copies[0].wait_recv()
                for copy in copies:
                    copy.start()

    def basis_last():
        @pl.when(is_src)
        def _():
            pltpu.make_async_copy(basis_v, own_v, bl).wait()
            for h in (0, 1):
                for copy in spread(h, 0, basis_v):
                    copy.wait_send()

        for h in (0, 1):
            copies = spread(h, 1, own_v)

            @pl.when(jnp.logical_not(member[h]))
            def _(copies=copies):
                copies[0].wait_recv()

            @pl.when(member[h])
            def _(copies=copies):
                for copy in copies:
                    copy.wait_send()

    exch = [[], []]

    def owner(k, core):
        return ((z + k) % NZ) * 2 + core

    def multiply(n):
        for lo in range(0, FF, 128 * 7):
            for at_, width in ((0, 256), (256, 256), (512, 256), (768, 128)):
                part = jnp.dot(
                    w[n], og_v[:, lo + at_ : lo + at_ + width], preferred_element_type=F32
                )
                top = 0 if lo == 0 else 8
                raw[n, :, top : top + 8, at_ : at_ + width] = part.reshape(16, 8, width)
        for i, (at_slot, count) in enumerate(PIECES):
            for k, slot in SLOT.items():
                if at_slot <= slot < at_slot + count:
                    cs[n, slot] = raw[n, owner(k, 1 - c)].astype(BF16)
            span = pl.ds(at_slot, count)
            exch[n].append(
                send(cs.at[n, span], cr.at[n, span], ces.at[n, i], cer.at[n, i], at(dc=1))
            )

    def chip_sum(k, n):
        return raw[n, owner(k, c)] + cr[n, SLOT[k]].astype(F32)

    reduced = [[], []]

    def reduce_start(n):
        for i, offsets in enumerate(((4, 3, 5), (2, 6), (1, 7))):
            exch[n][i].wait_recv()
            for k in offsets:
                tx[n, k - 1] = chip_sum(k, n).astype(BF16)
                reduced[n].append(
                    send(tx.at[n, k - 1], rx.at[n, k - 1], zs.at[n, k - 1], zr.at[n, k - 1], at(dz=k))
                )

    bias1 = 1.0 - B1**ADAM_STEP
    bias2 = 1.0 - B2**ADAM_STEP
    forwards, gathered = {}, {}

    def forward(n, off):
        block = up.at[n, ((z + off) % NZ) * 2 + c]
        forwards[n, off] = send(block, block, fs.at[n, off], fr.at[n, off], at(dc=1))

    def adam(n):
        for copy in reduced[n]:
            copy.wait_recv()
        grad = chip_sum(0, n)
        for k in range(NZ - 1):
            grad = grad + rx[n, k].astype(F32)
        grad = grad * scale
        first = B1 * side_by_side(m1_v, n) + (1.0 - B1) * grad
        second = B2 * side_by_side(m2_v, n) + (1.0 - B2) * grad * grad
        up[n, dp] = ((first / bias1) / (jnp.sqrt(second / bias2) + EPS)).astype(BF16)
        block = up.at[n, dp]
        for k in (4, 3, 5, 2, 6, 1, 7):
            gathered[n, k] = send(block, block, gs.at[n, k], gr.at[n, k], at(dz=k))
        forward(n, 0)
        for ref, value in ((nf_v, first), (ns_v, second)):
            ref[n * 8 : n * 8 + 8, 0:SIDE] = value[0:8]
            ref[n * 8 : n * 8 + 8, SIDE:FF] = value[8:16]

    for n in range(PARTS):
        for u in units_of(n):
            gather_end(u)
        if n == PARTS - 1:
            basis_first()
        multiply(n)
        reduce_start(n)
    basis_second()
    for n in range(PARTS):
        adam(n)
    for n in range(PARTS):
        for k in (1, 7, 2, 6, 3, 5, 4):
            gathered[n, k].wait_recv()
            forward(n, NZ - k)
    basis_last()
    for n in range(PARTS):
        for off in range(NZ):
            forwards[n, off].wait_recv()
    for copy in pending:
        copy.wait_send()


def final_kernel(nf_v, ns_v, own_v, up, nf_o, ns_o, wu_o, wu_v, osem):
    copies = [
        pltpu.make_async_copy(nf_v, nf_o, osem.at[0]),
        pltpu.make_async_copy(ns_v, ns_o, osem.at[1]),
    ]
    for copy in copies:
        copy.start()
    n = 2
    for h in (0, 1):
        for at_, width in ((0, 256), (256, 256), (512, 256), (768, 128)):
            lines = [
                up[i, :, :, at_ : at_ + width].astype(F32)[:, h * 8 : h * 8 + 8] for i in range(PARTS)
            ]
            lines = jnp.concatenate(lines, axis=1).astype(BF16).reshape(R, width)
            lo = h * SIDE + at_
            cols = pl.ds(lo, width)
            wu_v[:, lo : lo + width] = jnp.dot(
                own_v[...], lines, preferred_element_type=F32
            ).astype(BF16)
            copies.append(pltpu.make_async_copy(wu_v.at[:, cols], wu_o.at[:, cols], osem.at[n]))
            copies[-1].start()
            n += 1
    for copy in copies:
        copy.wait()


def local(activations, out_grads, basis, first_moment, second_moment, reward_codes, token_ids):
    hbm = pl.BlockSpec(memory_space=pltpu.HBM)
    near = pl.BlockSpec(memory_space=pltpu.VMEM)
    vm = pltpu.VMEM
    dma = pltpu.SemaphoreType.DMA
    moments = jax.ShapeDtypeStruct((ROWS, FF), F32)
    states = pl.pallas_call(
        kernel,
        out_shape=(
            vm((ROWS, FF), F32),
            vm((ROWS, FF), F32),
            vm((D, R), BF16),
            vm((PARTS, 16, ROWS, SIDE), BF16),
        ),
        in_specs=[hbm] * 7,
        out_specs=(near,) * 4,
        scratch_shapes=[
            vm((TOK, D), BF16), vm((TOK, FF), BF16), vm((D, R), BF16), vm((R, D), BF16),
            vm((ROWS, FF), F32), vm((ROWS, FF), F32),
            vm((TOK // 128, 128), jnp.int32), vm((TOK // 128, 128), jnp.int32),
            vm((ROWS, TOK), F32),
            vm((PARTS, RP, TOK), BF16), vm((PARTS, RP, TOK), BF16),
            vm((2 * PARTS, 3, BLK, HALF), BF16), vm((2 * PARTS, BLK, HALF), BF16),
            vm((2 * PARTS, 3, BLK, HALF), BF16), vm((PARTS, 16, ROWS, SIDE), F32),
            vm((2, 8, 128), F32), vm((8, 8, 128), F32),
            vm((PARTS, 8, ROWS, SIDE), BF16), vm((PARTS, 8, ROWS, SIDE), BF16),
            vm((PARTS, 8, ROWS, SIDE), BF16), vm((PARTS, 8, ROWS, SIDE), BF16),
            dma((13,)), dma((2 * PARTS, 9)), dma((2 * PARTS, 9)), dma((8,)), dma((8,)),
            dma((2, 3)), dma((2, 3)), dma((2, 8)), dma((2, 8)), dma((2, 8)), dma((2, 8)),
            dma((2, 8)), dma((2, 8)), dma((12,)), dma((2,)), dma,
        ],
        compiler_params=pltpu.CompilerParams(
            collective_id=0, has_side_effects=True, vmem_limit_bytes=55_260_000
        ),
        name="galore_step",
    )(
        activations, out_grads, basis, first_moment, second_moment,
        reward_codes.reshape(TOK // 128, 128), token_ids.reshape(TOK // 128, 128),
    )
    return pl.pallas_call(
        final_kernel,
        out_shape=(moments, moments, jax.ShapeDtypeStruct((D, FF), BF16)),
        in_specs=[near] * 4,
        out_specs=(hbm, hbm, hbm),
        scratch_shapes=[vm((D, FF), BF16), dma((10,))],
        compiler_params=pltpu.CompilerParams(vmem_limit_bytes=16 * 1024 * 1024),
        name="project_back",
    )(*states)


def solution(mesh):
    return jax.shard_map(
        local,
        mesh=mesh,
        in_specs=(
            P("dp", "tensor"),
            P("dp", "tensor"),
            P("tensor", None),
            P("dp", "tensor"),
            P("dp", "tensor"),
            P("dp"),
            P("dp"),
        ),
        out_specs=(P("dp", "tensor"), P("dp", "tensor"), P("dp", "tensor")),
        check_vma=False,
    )
```

time: 66.5 us -> 59.1 us (0.89)
  Pallas kernels: 65.7 us -> 58.4 us
    pallas_call x1, Pallas kernels: 64.1 us -> 56.8 us  [local(): pl.pallas_call(kernel, out_shape=(vm((ROWS, FF), F32), vm((ROWS, FF), F32...]
where the time goes in v3:
time: 59.1 us; the launch traced here: 59 us
  Pallas kernels  58.4 us (99%)
  between operations  0.64 us (1%)
    pallas_call x1, Pallas kernels, local(): pl.pallas_call(kernel, out_shape=(vm((ROWS, FF), F32), vm((ROWS, FF), F32...  56.8 us
    pallas_call x1, Pallas kernels, local(): pl.pallas_call(final_kernel, out_shape=(moments, moments, jax.ShapeDtypeS...  1.62 us

profile of v3, /device:TPU:1, one launch (start us, length us, event | category | flops | bytes accessed | tf_op | source)
XLA Modules:
  0.0 59.0 jit_solution(15197481392256693877)
XLA Ops:
  0.6 56.8 %galore_step.1 = (f32[16,1792]{1,0:T(8,128)S(1)}, f32[16,1792]{1,0:T(8,128)S(1)}, bf16[512,256]{1,0:T(8,128)(2,1)S(1)}, bf16[2,16,16,896]{3,2,1,0:T(8,128)(2,1)S(1)}) custom-call(bf16[2304,512]{1,0:T(8,128)(2,1)} %act.1, bf16[2304,1792]{1,0:T(8,128)(2,1)} %og.1, bf16[512,256]{1,0:T(8,128)(2,1)} %basis.1, f32[16,1792]{1,0:T(8,128)} %m1.1, f32[16,1792]{1,0:T(8,128)} %m2.1, ...), custom_call_target="tpu_custom_call" | custom-call | tf_op jit(solution)/shard_map/galore_step/pallas_call | solution.py:382
  57.4 1.6 %project_back.1 = (f32[16,1792]{1,0:T(8,128)}, f32[16,1792]{1,0:T(8,128)}, bf16[512,1792]{1,0:T(8,128)(2,1)}) custom-call(f32[16,1792]{1,0:T(8,128)S(1)} %get-tuple-element.7.nf_v, f32[16,1792]{1,0:T(8,128)S(1)} %get-tuple-element.8.ns_v, bf16[512,256]{1,0:T(8,128)(2,1)S(1)} %get-tuple-element.9.own_v, bf16[2,16,16,896]{3,2,1,0:T(8,128)(2,1)S(1)} %get-tuple-element.10.up), custom_call_target="tpu_custom_call" | custom-call | tf_op jit(solution)/shard_map/project_back/pallas_call | solution.py:415

commit v4 on v3

--- a/solution.py
+++ b/solution.py
@@ -29,6 +29,9 @@
 SIDE = FF // 2
 TOKENS = TOK * 16
 SLOT = {4: 0, 3: 1, 5: 2, 2: 3, 6: 4, 1: 5, 7: 6, 0: 7}
+LEFT, RIGHT = pl.ds(0, 512), pl.ds(512, SIDE - 512)
+SUM_RELAY = (0, 1)
+GATHER_RELAY = (0, 1)
 PIECES = ((0, 3), (3, 2), (5, 3))
 
 
@@ -103,15 +106,17 @@
     turned = basis_v[...].astype(F32).T.reshape(16, PARTS, 8, D)
     for n in range(PARTS):
         basis_t[n * RP : (n + 1) * RP, :] = turned[:, n].reshape(RP, D).astype(BF16)
-    for i in range(6):
-        f_act[i].wait()
-        part = lax.dot_general(
-            basis_t[...], act_v[i * step : (i + 1) * step, :],
-            (((1,), (1,)), ((), ())), preferred_element_type=F32,
-        ).astype(BF16)
-        for n in range(PARTS):
-            p[n, :, i * step : (i + 1) * step] = part[n * RP : (n + 1) * RP, :]
-
+    for copy in f_act:
+        copy.wait()
+
+    def project(n):
+        for i in range(6):
+            p[n, :, i * step : (i + 1) * step] = lax.dot_general(
+                basis_t[n * RP : (n + 1) * RP, :], act_v[i * step : (i + 1) * step, :],
+                (((1,), (1,)), ((), ())), preferred_element_type=F32,
+            ).astype(BF16)
+
+    project(0)
     pl.semaphore_wait(barrier, len(partners))
 
     class Unit:
@@ -169,7 +174,10 @@
     def units_of(n):
         return units[2 * n : 2 * n + 2]
 
-    for u in units:
+    for u in units_of(0):
+        scatter_start(u)
+    project(1)
+    for u in units_of(1):
         scatter_start(u)
 
     f_codes.wait()
@@ -290,6 +298,38 @@
 
     reduced = [[], []]
 
+    def reduce_send(n, k, to, sem, cols=slice(None)):
+        return send(
+            tx.at[n, k - 1, :, cols], rx.at[n, k - 1, :, cols], zs.at[n, sem], zr.at[n, sem], at(dz=to)
+        )
+
+    relayed = {}
+
+    def reduce_start_relayed(n):
+        exch[n][0].wait_recv()
+        for k in (4, 3, 5):
+            tx[n, k - 1] = chip_sum(k, n).astype(BF16)
+            if k == 4:
+                relayed[n, "a"] = reduce_send(n, 4, 2, 3, LEFT)
+                relayed[n, "b"] = reduce_send(n, 4, 6, 7, RIGHT)
+            else:
+                relayed[n, k] = reduce_send(n, k, 1 if k == 3 else 7, k - 1)
+        exch[n][1].wait_recv()
+        exch[n][2].wait_recv()
+        for k in (1, 7):
+            tx[n, k - 1] = chip_sum(k, n).astype(BF16)
+            reduced[n].append(reduce_send(n, k, k, k - 1))
+
+    def reduce_relay(n):
+        for k, near, far, cols in ((2, 3, "a", LEFT), (6, 5, "b", RIGHT)):
+            relayed[n, near].wait_recv()
+            relayed[n, far].wait_recv()
+            total = chip_sum(k, n) + rx[n, near - 1].astype(F32)
+            tx[n, k - 1] = total.astype(BF16)
+            more = total[:, cols.start : cols.start + cols.size] + rx[n, 3, :, cols].astype(F32)
+            tx[n, k - 1, :, cols] = more.astype(BF16)
+            reduced[n].append(reduce_send(n, k, k, k - 1))
+
     def reduce_start(n):
         for i, offsets in enumerate(((4, 3, 5), (2, 6), (1, 7))):
             exch[n][i].wait_recv()
@@ -307,18 +347,28 @@
         block = up.at[n, ((z + off) % NZ) * 2 + c]
         forwards[n, off] = send(block, block, fs.at[n, off], fr.at[n, off], at(dc=1))
 
+    def gather_relay(n):
+        for k, near, half, cols in ((2, 3, 4, LEFT), (6, 5, 0, RIGHT)):
+            gathered[n, k].wait_recv()
+            block = up.at[n, ((z + NZ - k) % NZ) * 2 + c]
+            part = up.at[n, ((z + NZ - k) % NZ) * 2 + c, :, cols]
+            gathered[n, half] = send(part, part, gs.at[n, half], gr.at[n, half], at(dz=k))
+            gathered[n, near] = send(
+                block, block, gs.at[n, near], gr.at[n, near], at(dz=1 if k == 2 else NZ - 1)
+            )
+
     def adam(n):
         for copy in reduced[n]:
             copy.wait_recv()
         grad = chip_sum(0, n)
-        for k in range(NZ - 1):
+        for k in (0, 1, 5, 6) if n in SUM_RELAY else range(NZ - 1):
             grad = grad + rx[n, k].astype(F32)
         grad = grad * scale
         first = B1 * side_by_side(m1_v, n) + (1.0 - B1) * grad
         second = B2 * side_by_side(m2_v, n) + (1.0 - B2) * grad * grad
         up[n, dp] = ((first / bias1) / (jnp.sqrt(second / bias2) + EPS)).astype(BF16)
         block = up.at[n, dp]
-        for k in (4, 3, 5, 2, 6, 1, 7):
+        for k in (2, 6, 1, 7) if n in GATHER_RELAY else (4, 3, 5, 2, 6, 1, 7):
             gathered[n, k] = send(block, block, gs.at[n, k], gr.at[n, k], at(dz=k))
         forward(n, 0)
         for ref, value in ((nf_v, first), (ns_v, second)):
@@ -328,17 +378,38 @@
     for n in range(PARTS):
         for u in units_of(n):
             gather_end(u)
-        if n == PARTS - 1:
-            basis_first()
         multiply(n)
-        reduce_start(n)
+        if n in SUM_RELAY:
+            reduce_start_relayed(n)
+        else:
+            reduce_start(n)
+    basis_first()
+    for n in range(PARTS):
+        if n in SUM_RELAY:
+            reduce_relay(n)
+    for n in range(PARTS):
+        adam(n)
     basis_second()
     for n in range(PARTS):
-        adam(n)
-    for n in range(PARTS):
-        for k in (1, 7, 2, 6, 3, 5, 4):
-            gathered[n, k].wait_recv()
-            forward(n, NZ - k)
+        if n in GATHER_RELAY:
+            gather_relay(n)
+    for n in range(PARTS):
+        if n in GATHER_RELAY:
+            for k in (1, 7):
+                gathered[n, k].wait_recv()
+                forward(n, NZ - k)
+            for k in (2, 6):
+                forward(n, NZ - k)
+            for k in (3, 5):
+                gathered[n, k].wait_recv()
+                forward(n, NZ - k)
+            gathered[n, 4].wait_recv()
+            gathered[n, 0].wait_recv()
+            forward(n, 4)
+        else:
+            for k in (1, 7, 2, 6, 3, 5, 4):
+                gathered[n, k].wait_recv()
+                forward(n, NZ - k)
     basis_last()
     for n in range(PARTS):
         for off in range(NZ):

time: 59.1 us -> 55.6 us (0.941)
  Pallas kernels: 58.4 us -> 54.9 us
    pallas_call x1, Pallas kernels: 56.8 us -> 53.3 us  [local(): pl.pallas_call(kernel, out_shape=(vm((ROWS, FF), F32), vm((ROWS, FF), F32...]
where the time goes in v4:
time: 55.6 us; the launch traced here: 55.5 us
  Pallas kernels  54.9 us (99%)
  between operations  0.64 us (1%)
    pallas_call x1, Pallas kernels, local(): pl.pallas_call(kernel, out_shape=(vm((ROWS, FF), F32), vm((ROWS, FF), F32...  53.3 us
    pallas_call x1, Pallas kernels, local(): pl.pallas_call(final_kernel, out_shape=(moments, moments, jax.ShapeDtypeS...  1.62 us

profile of v4, /device:TPU:1, one launch (start us, length us, event | category | flops | bytes accessed | tf_op | source)
XLA Modules:
  0.0 55.5 jit_solution(8415629144008798711)
XLA Ops:
  0.6 53.3 %galore_step.1 = (f32[16,1792]{1,0:T(8,128)S(1)}, f32[16,1792]{1,0:T(8,128)S(1)}, bf16[512,256]{1,0:T(8,128)(2,1)S(1)}, bf16[2,16,16,896]{3,2,1,0:T(8,128)(2,1)S(1)}) custom-call(bf16[2304,512]{1,0:T(8,128)(2,1)} %act.1, bf16[2304,1792]{1,0:T(8,128)(2,1)} %og.1, bf16[512,256]{1,0:T(8,128)(2,1)} %basis.1, f32[16,1792]{1,0:T(8,128)} %m1.1, f32[16,1792]{1,0:T(8,128)} %m2.1, ...), custom_call_target="tpu_custom_call" | custom-call | tf_op jit(solution)/shard_map/galore_step/pallas_call | solution.py:453
  53.9 1.6 %project_back.1 = (f32[16,1792]{1,0:T(8,128)}, f32[16,1792]{1,0:T(8,128)}, bf16[512,1792]{1,0:T(8,128)(2,1)}) custom-call(f32[16,1792]{1,0:T(8,128)S(1)} %get-tuple-element.7.nf_v, f32[16,1792]{1,0:T(8,128)S(1)} %get-tuple-element.8.ns_v, bf16[512,256]{1,0:T(8,128)(2,1)S(1)} %get-tuple-element.9.own_v, bf16[2,16,16,896]{3,2,1,0:T(8,128)(2,1)S(1)} %get-tuple-element.10.up), custom_call_target="tpu_custom_call" | custom-call | tf_op jit(solution)/shard_map/project_back/pallas_call | solution.py:486

commit v5 on v4

--- a/solution.py
+++ b/solution.py
@@ -82,6 +82,11 @@
         pending.append(copy)
         return copy
 
+    def drain(count):
+        for copy in pending[:count]:
+            copy.wait_send()
+        del pending[:count]
+
     def fetch(src, dst, n):
         copy = pltpu.make_async_copy(src, dst, lsem.at[n])
         copy.start()
@@ -379,17 +384,21 @@
         for u in units_of(n):
             gather_end(u)
         multiply(n)
+        early = len(pending)
         if n in SUM_RELAY:
             reduce_start_relayed(n)
         else:
             reduce_start(n)
     basis_first()
+    drain(early)
+    early = len(pending)
     for n in range(PARTS):
         if n in SUM_RELAY:
             reduce_relay(n)
     for n in range(PARTS):
         adam(n)
     basis_second()
+    drain(early)
     for n in range(PARTS):
         if n in GATHER_RELAY:
             gather_relay(n)

time: 55.6 us -> 55.5 us (level)
  no operation moved by 1% of the time
where the time goes in v5:
time: 55.5 us; the launch traced here: 55.4 us
  Pallas kernels  54.8 us (99%)
  between operations  0.64 us (1%)
    pallas_call x1, Pallas kernels, local(): pl.pallas_call(kernel, out_shape=(vm((ROWS, FF), F32), vm((ROWS, FF), F32...  53.2 us
    pallas_call x1, Pallas kernels, local(): pl.pallas_call(final_kernel, out_shape=(moments, moments, jax.ShapeDtypeS...  1.62 us

profile of v5, /device:TPU:1, one launch (start us, length us, event | category | flops | bytes accessed | tf_op | source)
XLA Modules:
  0.0 55.4 jit_solution(10298298073464913652)
XLA Ops:
  0.6 53.2 %galore_step.1 = (f32[16,1792]{1,0:T(8,128)S(1)}, f32[16,1792]{1,0:T(8,128)S(1)}, bf16[512,256]{1,0:T(8,128)(2,1)S(1)}, bf16[2,16,16,896]{3,2,1,0:T(8,128)(2,1)S(1)}) custom-call(bf16[2304,512]{1,0:T(8,128)(2,1)} %act.1, bf16[2304,1792]{1,0:T(8,128)(2,1)} %og.1, bf16[512,256]{1,0:T(8,128)(2,1)} %basis.1, f32[16,1792]{1,0:T(8,128)} %m1.1, f32[16,1792]{1,0:T(8,128)} %m2.1, ...), custom_call_target="tpu_custom_call" | custom-call | tf_op jit(solution)/shard_map/galore_step/pallas_call | solution.py:462
  53.8 1.6 %project_back.1 = (f32[16,1792]{1,0:T(8,128)}, f32[16,1792]{1,0:T(8,128)}, bf16[512,1792]{1,0:T(8,128)(2,1)}) custom-call(f32[16,1792]{1,0:T(8,128)S(1)} %get-tuple-element.7.nf_v, f32[16,1792]{1,0:T(8,128)S(1)} %get-tuple-element.8.ns_v, bf16[512,256]{1,0:T(8,128)(2,1)S(1)} %get-tuple-element.9.own_v, bf16[2,16,16,896]{3,2,1,0:T(8,128)(2,1)S(1)} %get-tuple-element.10.up), custom_call_target="tpu_custom_call" | custom-call | tf_op jit(solution)/shard_map/project_back/pallas_call | solution.py:495
